TPU v7x, 128 devices: a whole 4x4x4 slice. The times are simulated.
128 devices in a mesh: grp: 8 (over z_hi, y), seq: 16 (over x, z_lo, core).
Axes of the slice: x: 4, y: 4, z: 4 (z_hi: 2, z_lo: 2; z = z_hi * 2 + z_lo), core: 2. Of those that a mesh axis runs over, the one named last changes fastest.
Arguments:
- queries: bfloat16 [128, 1024, 1024], P(('grp', 'seq')), may hold values from -12 to 12
- key_vectors: bfloat16 [128, 1024, 1024], P(('grp', 'seq')), may hold values from -6 to 6
- value_vectors: bfloat16 [128, 1024, 1024], P(('grp', 'seq')), may hold values from -6 to 6
- out_cotangent: bfloat16 [128, 1024, 1024], P(('grp', 'seq')), may hold values from -6 to 6
Outputs:
- attended: bfloat16 [128, 1024, 1024], P(('grp', 'seq'))
- query_grad: bfloat16 [128, 1024, 1024], P(('grp', 'seq'))
- key_grad: bfloat16 [128, 1024, 1024], P(('grp', 'seq'))
- value_grad: bfloat16 [128, 1024, 1024], P(('grp', 'seq'))
All inputs are finite; a program needn't handle non-finite values.
Results may differ from a plain program's by a relative error of at most 0.028.
Values may be sent and summed in bfloat16 or wider, within the bound.
No kernel may reach another device: no remote copies, remote signals or barrier semaphores. Data moves between devices by JAX's collectives and lax.ppermute only.
A program may use at most 192 MiB of HBM per device.

v0:
```python
import functools
import itertools
import math

import jax
import jax.numpy as jnp
from jax import lax
from jax.experimental import pallas as pl
from jax.experimental.pallas import tpu as pltpu
from jax.sharding import PartitionSpec as P

HEADS = 8
HDIM = 128
HALF = HEADS // 2
SCALING = HDIM ** (-0.5)
LOG2E = math.log2(math.e)
NEG = -1e30
AHEAD = 1000
PIECES = 4
CHUNKS = 4
VMEM_BYTES = 64 * 1024 * 1024 - 256 * 1024
AXES = ("grp", "seq")
F32 = jnp.float32
BF16 = jnp.bfloat16


def matmul(lhs, rhs):
    return jnp.dot(lhs, rhs, preferred_element_type=F32)


def matmul_nt(lhs, rhs):
    return lax.dot_general(lhs, rhs, (((1,), (1,)), ((), ())), preferred_element_type=F32)


def matmul_tn(lhs, rhs):
    return lax.dot_general(lhs, rhs, (((0,), (0,)), ((), ())), preferred_element_type=F32)


def params():
    return pltpu.CompilerParams(vmem_limit_bytes=VMEM_BYTES)


def stream(moves, in_sems, out_sems):
    arriving = []
    for incoming, _ in moves:
        started = []
        for source, target in incoming:
            started.append(pltpu.make_async_copy(source, target, in_sems.at[len(arriving), len(started)]))
            started[-1].start()
        arriving.append(started)
    leaving = []
    for at, (_, outgoing) in enumerate(moves):
        for copy in arriving[at]:
            copy.wait()
        for source, target in outgoing:
            copy = pltpu.make_async_copy(source, target, out_sems.at[at, len(leaving) % len(outgoing)])
            copy.start()
            leaving.append(copy)
    for copy in leaving:
        copy.wait()


def pair_kernel(first, k_ref, v_ref, *refs):
    outs, (buffer, in_sems, out_sems) = refs[:-3], refs[-3:]
    wide = outs[0].shape[2]
    moves = []
    for piece, out in enumerate(outs):
        here = pl.ds(first * HDIM + piece * wide, wide)
        incoming = [
            (ref.at[0, :, here], buffer.at[piece, at]) for at, ref in enumerate((k_ref, v_ref))
        ]
        moves.append((incoming, [(buffer.at[piece], out)]))
    stream(moves, in_sems, out_sems)


def pack_pairs(key_vectors, value_vectors, first, pieces):
    _, length, width = key_vectors.shape
    wide = width // 2 // PIECES
    anywhere = pl.BlockSpec(memory_space=pl.ANY)
    return pl.pallas_call(
        functools.partial(pair_kernel, first),
        in_specs=[anywhere] * 2,
        out_specs=[anywhere] * pieces,
        out_shape=[jax.ShapeDtypeStruct((2, length, wide), BF16)] * pieces,
        scratch_shapes=[
            pltpu.VMEM((pieces, 2, length, wide), BF16),
            pltpu.SemaphoreType.DMA((pieces, 2)),
            pltpu.SemaphoreType.DMA((pieces, 1)),
        ],
        compiler_params=params(),
        cost_estimate=pl.CostEstimate(
            flops=0, bytes_accessed=8 * pieces * length * wide, transcendentals=0
        ),
        name="pack_pairs",
    )(key_vectors, value_vectors)


def pack_kernel(q_ref, k_ref, v_ref, g_ref, out_ref, buffer, in_sems, out_sems):
    devices, _, per, half = out_ref.shape
    count = devices // CHUNKS
    moves = []
    for chunk in range(CHUNKS):
        part = pl.ds(chunk * count, count)
        incoming = [
            (ref.at[part, :, pl.ds(half, half)], buffer.at[part, at])
            for at, ref in enumerate((q_ref, k_ref, v_ref, g_ref))
        ]
        moves.append((incoming, [(buffer.at[part], out_ref.at[part])]))
    stream(moves, in_sems, out_sems)


def pack_columns(arrays, devices):
    _, length, width = arrays[0].shape
    half = width // 2
    per = length // devices
    anywhere = pl.BlockSpec(memory_space=pl.ANY)
    shape = (devices, 4, per, half)
    return pl.pallas_call(
        pack_kernel,
        in_specs=[anywhere] * 4,
        out_specs=anywhere,
        out_shape=jax.ShapeDtypeStruct(shape, BF16),
        scratch_shapes=[
            pltpu.VMEM(shape, BF16),
            pltpu.SemaphoreType.DMA((CHUNKS, 4)),
            pltpu.SemaphoreType.DMA((CHUNKS, 1)),
        ],
        compiler_params=params(),
        cost_estimate=pl.CostEstimate(
            flops=0, bytes_accessed=16 * length * half, transcendentals=0
        ),
        name="pack_columns",
    )(*[array.reshape(devices, per, width) for array in arrays])


def row_kernel(block, made, bias_ref, q_ref, k_ref, v_ref, g_ref, prior_ref, *refs):
    out_ref, dq_ref, dk_ref, dv_ref, dk_prior, dv_prior = refs[made : made + 6]
    keys, values, keys_t, values_t, scores, dkeys, dvalues = refs[made + 6 :]
    length = q_ref.shape[1]
    window = length + block
    parts = window // block
    keys[:length] = prior_ref[0]
    keys[length:] = k_ref[0]
    values[:length] = prior_ref[1]
    values[length:] = v_ref[0]
    for at in range(0, 2 * length, block):
        rows = slice(at, at + block)
        keys_t[:, rows] = keys[rows].T
        values_t[:, rows] = values[rows].T
    dkeys[...] = jnp.zeros_like(dkeys)
    dvalues[...] = jnp.zeros_like(dvalues)
    bias = bias_ref[0]
    key_at = lax.broadcasted_iota(jnp.int32, (block, block), 0)
    query_at = lax.broadcasted_iota(jnp.int32, (block, block), 1)
    older = key_at > query_at
    for qi in range(length // block):
        here = slice(qi * block, (qi + 1) * block)
        query = q_ref[0, here]
        grad = g_ref[0, here]
        query_t = query.T
        grad_t = grad.T

        def rows_of(part):
            start = qi * block + part * block
            return slice(start, start + block)

        def is_prior(part):
            return (qi + part) * block < length

        peak = jnp.full((1, block), NEG, F32)
        for part in range(parts):
            score = matmul(keys[rows_of(part)], query_t)
            if part == 0:
                score = jnp.where(older, score, NEG)
            if part == parts - 1:
                score = jnp.where(older, NEG, score)
            top = jnp.max(score, axis=0, keepdims=True)
            if is_prior(part):
                top = top + bias
            peak = jnp.maximum(peak, top)
            scores[part * block : (part + 1) * block] = score
        factor = SCALING * LOG2E
        scaled_peak = peak * factor
        shifted_prior = (peak - bias) * factor
        total = jnp.zeros((1, block), F32)
        for part in range(parts):
            rows = slice(part * block, (part + 1) * block)
            shift = shifted_prior if is_prior(part) else scaled_peak
            weight = jnp.exp2(scores[rows] * factor - shift)
            total = total + jnp.sum(weight, axis=0, keepdims=True)
            scores[rows] = weight
        inverse = 1.0 / total
        attended = jnp.zeros((HDIM, block), F32)
        for part in range(parts):
            rows = slice(part * block, (part + 1) * block)
            weight = scores[rows].astype(BF16)
            attended = attended + matmul(values_t[:, rows_of(part)], weight)
        attended = (attended * inverse).astype(BF16)
        out_ref[0, here] = attended.T
        row_dot = jnp.sum(
            attended.astype(F32) * grad_t.astype(F32), axis=0, keepdims=True
        )
        query_grad = jnp.zeros((HDIM, block), F32)
        for part in range(parts):
            rows = slice(part * block, (part + 1) * block)
            probability = scores[rows] * inverse
            dprob = matmul(values[rows_of(part)], grad_t)
            dscore = (probability * (dprob - row_dot)).astype(BF16)
            query_grad = query_grad + matmul(keys_t[:, rows_of(part)], dscore)
            dkeys[rows_of(part)] += matmul(dscore, query)
            dvalues[rows_of(part)] += matmul(probability.astype(BF16), grad)
        dq_ref[0, here] = (query_grad * SCALING).astype(BF16).T
    dk_ref[0] = (dkeys[length:] * SCALING).astype(BF16)
    dv_ref[0] = dvalues[length:].astype(BF16)
    dk_prior[0] = (dkeys[:length] * SCALING).astype(BF16)
    dv_prior[0] = dvalues[:length].astype(BF16)


def row_heads(piece, bias, arrays, prior, made):
    _, length, width = arrays[0].shape
    block = 256
    window = length + block
    heads = HALF // PIECES
    one = pl.BlockSpec((1, length, HDIM), lambda h: (0, 0, piece * heads + h))
    two = pl.BlockSpec((2, length, HDIM), lambda h: (0, 0, h))
    shape = jax.ShapeDtypeStruct((1, length, width), BF16)
    partial_shape = jax.ShapeDtypeStruct((1, length, HALF * HDIM), BF16)
    return pl.pallas_call(
        functools.partial(row_kernel, block, len(made)),
        grid=(heads,),
        in_specs=[pl.BlockSpec(memory_space=pltpu.SMEM)]
        + [one] * 4
        + [two]
        + [pl.BlockSpec(memory_space=pl.ANY)] * len(made),
        out_specs=[one] * 6,
        out_shape=[shape] * 4 + [partial_shape] * 2,
        input_output_aliases={6 + at: at for at in range(len(made))},
        scratch_shapes=[
            pltpu.VMEM((2 * length, HDIM), BF16),
            pltpu.VMEM((2 * length, HDIM), BF16),
            pltpu.VMEM((HDIM, 2 * length), BF16),
            pltpu.VMEM((HDIM, 2 * length), BF16),
            pltpu.VMEM((window, block), F32),
            pltpu.VMEM((2 * length, HDIM), F32),
            pltpu.VMEM((2 * length, HDIM), F32),
        ],
        compiler_params=params(),
        cost_estimate=pl.CostEstimate(
            flops=AHEAD * heads * length * window * HDIM,
            bytes_accessed=24 * heads * length * HDIM,
            transcendentals=heads * length * window,
        ),
        name="row_heads",
    )(bias, *arrays, prior, *made)


def column_kernel(row_down, row_across, in_ref, out_ref, *scratch):
    rows, _, per, _ = in_ref.shape
    staged, results = scratch[:4], scratch[4:]
    for at, ref in enumerate(staged):
        ref[...] = in_ref[:, at].astype(F32).reshape(rows * per, HDIM)
    causal = row_down[...] <= row_across[...]
    factor = SCALING * LOG2E
    columns = range(per)
    picks = [pl.ds(column, rows, stride=per) for column in columns]
    query, key, value, grad = [
        [ref[pick, :].astype(BF16) for pick in picks] for ref in staged
    ]
    score = [jnp.where(causal, matmul_nt(key[c], query[c]), NEG) for c in columns]
    dprob = [matmul_nt(value[c], grad[c]) for c in columns]
    peak = [jnp.max(score[c], axis=0, keepdims=True) for c in columns]
    weight = [jnp.exp2((score[c] - peak[c]) * factor) for c in columns]
    inverse = [1.0 / jnp.sum(weight[c], axis=0, keepdims=True) for c in columns]
    probability = [weight[c] * inverse[c] for c in columns]
    low = [probability[c].astype(BF16) for c in columns]
    row_dot = [jnp.sum(probability[c] * dprob[c], axis=0, keepdims=True) for c in columns]
    dscore = [(probability[c] * (dprob[c] - row_dot[c])).astype(BF16) for c in columns]
    for c in columns:
        results[0][picks[c], :] = matmul_tn(low[c], value[c])
    for c in columns:
        results[3][picks[c], :] = matmul(low[c], grad[c])
    for c in columns:
        results[1][picks[c], :] = matmul_tn(dscore[c], key[c]) * SCALING
    for c in columns:
        results[2][picks[c], :] = matmul(dscore[c], query[c]) * SCALING
    for at, ref in enumerate(results):
        out_ref[:, at] = ref[...].reshape(rows, per, HDIM).astype(BF16)


def column_heads(arrived, order):
    rows, _, per, half = arrived.shape
    row_ids = jnp.array(order, jnp.int32)
    spec = pl.BlockSpec((rows, 4, per, HDIM), lambda h: (0, 0, 0, h))
    return pl.pallas_call(
        column_kernel,
        grid=(HALF,),
        in_specs=[
            pl.BlockSpec((rows, 1), lambda h: (0, 0)),
            pl.BlockSpec((1, rows), lambda h: (0, 0)),
            spec,
        ],
        out_specs=spec,
        out_shape=jax.ShapeDtypeStruct(arrived.shape, BF16),
        scratch_shapes=[pltpu.VMEM((rows * per, HDIM), F32)] * 8,
        compiler_params=params(),
        cost_estimate=pl.CostEstimate(
            flops=12 * HALF * per * rows * rows * HDIM,
            bytes_accessed=16 * rows * per * half,
            transcendentals=HALF * per * rows * rows,
        ),
        name="column_heads",
    )(row_ids[:, None], row_ids[None, :], arrived)


def add_kernel(dk_back, dv_back, dk_in, dv_in, dk_ref, dv_ref):
    dk_ref[0] = (dk_in[0].astype(F32) + dk_back[0].astype(F32)).astype(BF16)
    dv_ref[0] = (dv_in[0].astype(F32) + dv_back[0].astype(F32)).astype(BF16)


def add_returned(back, row_dk, row_dv):
    _, length, half = back[0].shape
    rows = 512
    left = pl.BlockSpec((1, rows, half), lambda i: (0, i, 0))
    shape = jax.ShapeDtypeStruct(row_dk.shape, BF16)
    return pl.pallas_call(
        add_kernel,
        grid=(length // rows,),
        in_specs=[left] * 4,
        out_specs=[left, left],
        out_shape=[shape] * 2,
        input_output_aliases={2: 0, 3: 1},
        compiler_params=params(),
        cost_estimate=pl.CostEstimate(
            flops=100 * AHEAD * length * HDIM * HDIM,
            bytes_accessed=12 * length * half,
            transcendentals=0,
        ),
        name="add_returned",
    )(*back, row_dk, row_dv)


def place_kernel(cols_ref, *refs):
    outs, (buffer, in_sems, out_sems) = refs[4:8], refs[8:]
    devices, _, per, half = cols_ref.shape
    count = devices // CHUNKS
    moves = []
    for chunk in range(CHUNKS):
        part = pl.ds(chunk * count, count)
        outgoing = [
            (buffer.at[part, at], out.at[part, :, pl.ds(half, half)])
            for at, out in enumerate(outs)
        ]
        moves.append(([(cols_ref.at[part], buffer.at[part])], outgoing))
    stream(moves, in_sems, out_sems)


def place(columns, rowwise):
    devices, _, per, half = columns.shape
    whole = rowwise[0].shape
    shape = (devices, per, whole[2])
    anywhere = pl.BlockSpec(memory_space=pl.ANY)
    placed = pl.pallas_call(
        place_kernel,
        in_specs=[anywhere] * 5,
        out_specs=[anywhere] * 4,
        out_shape=[jax.ShapeDtypeStruct(shape, BF16)] * 4,
        input_output_aliases={1: 0, 2: 1, 3: 2, 4: 3},
        scratch_shapes=[
            pltpu.VMEM(columns.shape, BF16),
            pltpu.SemaphoreType.DMA((CHUNKS, 1)),
            pltpu.SemaphoreType.DMA((CHUNKS, 4)),
        ],
        compiler_params=params(),
        cost_estimate=pl.CostEstimate(
            flops=0, bytes_accessed=16 * devices * per * half, transcendentals=0
        ),
        name="place",
    )(columns, *[array.reshape(shape) for array in rowwise])
    return [array.reshape(whole) for array in placed]


def exchange_order():
    order = []
    for z_hi, z_lo, y, x, core in itertools.product(range(2), range(2), range(4), range(4), range(2)):
        order.append(((z_hi * 4 + y) * 4 + x) * 4 + z_lo * 2 + core)
    return order


def exchange(blocks, order):
    return lax.all_to_all(
        blocks, AXES, split_axis=0, concat_axis=0, axis_index_groups=[order], tiled=True
    )


def on_device(queries, key_vectors, value_vectors, out_cotangent):
    devices = lax.axis_size(AXES)
    order = exchange_order()
    arrays = (queries, key_vectors, value_vectors, out_cotangent)
    forward = [(i, i + 1) for i in range(devices - 1)]
    backward = [(i + 1, i) for i in range(devices - 1)]
    last = PIECES - 1
    pairs = pack_pairs(key_vectors, value_vectors, 0, last)
    prior = [lax.ppermute(pair, AXES, forward) for pair in pairs]
    keys, values, _ = lax.optimization_barrier((key_vectors, value_vectors, prior[0]))
    pair = pack_pairs(keys, values, last * (HALF // PIECES), 1)[0]
    prior.append(lax.ppermute(pair, AXES, forward))
    packed = pack_columns(arrays, devices)
    packed, _ = lax.optimization_barrier((packed, prior[0]))
    arrived = exchange(packed, order)
    at_start = lax.axis_index(AXES) == 0
    bias = jnp.where(at_start, NEG, 0.0).astype(F32).reshape(1)
    made = ()
    for piece in range(PIECES):
        made = row_heads(piece, bias, arrays, prior[piece], made)
    row_out, row_dq, row_dk, row_dv, *partials = made
    arrived, *partials = lax.optimization_barrier((arrived, *partials))
    back = [lax.ppermute(partial, AXES, backward) for partial in partials]
    leaving = column_heads(arrived, order)
    leaving, _ = lax.optimization_barrier((leaving, back[0]))
    returned = exchange(leaving, order)
    row_dk, row_dv = add_returned(back, row_dk, row_dv)
    return tuple(place(returned, (row_out, row_dq, row_dk, row_dv)))


def solution(mesh):
    spec = P(AXES, None, None)
    return jax.shard_map(
        on_device, mesh=mesh, in_specs=(spec,) * 4, out_specs=(spec,) * 4, check_vma=False
    )
```

profile of v0, /device:TPU:1, one launch (start us, length us, event | category | flops | bytes accessed | tf_op | source)
XLA Modules:
  0.0 165.6 jit_solution(15363274783513120980)
XLA Ops:
  0.6 2.3 %pack_pairs.2 = (bf16[2,1024,128]{2,1,0:T(8,128)(2,1)}, bf16[2,1024,128]{2,1,0:T(8,128)(2,1)}, bf16[2,1024,128]{2,1,0:T(8,128)(2,1)}) custom-call(bf16[1,1024,1024]{2,1,0:T(8,128)(2,1)} %k_ref.10, bf16[1,1024,1024]{2,1,0:T(8,128)(2,1)} %v_ref.10), custom_call_target="tpu_custom_call" | custom-call | bytes 3145728 | tf_op jit(solution)/shard_map/pack_pairs/pallas_call | solution.py:80
  2.9 4.9 %collective-permute-start = (bf16[2,1024,128]{2,1,0:T(8,128)(2,1)}, bf16[2,1024,128]{2,1,0:T(8,128)(2,1)}, u32[]{:S(2)}, u32[]{:S(2)}) collective-permute-start(bf16[2,1024,128]{2,1,0:T(8,128)(2,1)} %get-tuple-element.44), channel_id=1, source_target_pairs={{0,1},{1,2},{2,3},{3,4},{4,5},{5,6},{6,7},{7,8},{8,9},{9,10},{10,1... | collective-permute-start | bytes 1572872 | tf_op jit(solution)/shard_map/ppermute | solution.py:403
  7.9 1.9 %collective-permute-start.3 = (bf16[2,1024,128]{2,1,0:T(8,128)(2,1)}, bf16[2,1024,128]{2,1,0:T(8,128)(2,1)}, u32[]{:S(2)}, u32[]{:S(2)}) collective-permute-start(bf16[2,1024,128]{2,1,0:T(8,128)(2,1)} %get-tuple-element.49), channel_id=1, source_target_pairs={{0,1},{1,2},{2,3},{3,4},{4,5},{5,6},{6,7},{7,8},{8,9},{9,10},{10,1... | collective-permute-start | bytes 1572872 | tf_op jit(solution)/shard_map/ppermute | solution.py:403
  9.8 3.0 %collective-permute-start.2 = (bf16[2,1024,128]{2,1,0:T(8,128)(2,1)}, bf16[2,1024,128]{2,1,0:T(8,128)(2,1)}, u32[]{:S(2)}, u32[]{:S(2)}) collective-permute-start(bf16[2,1024,128]{2,1,0:T(8,128)(2,1)} %get-tuple-element.48), channel_id=1, source_target_pairs={{0,1},{1,2},{2,3},{3,4},{4,5},{5,6},{6,7},{7,8},{8,9},{9,10},{10,1... | collective-permute-start | bytes 1572872 | tf_op jit(solution)/shard_map/ppermute | solution.py:403
  12.9 3.5 %pack_columns.1 = bf16[128,4,8,512]{3,2,1,0:T(8,128)(2,1)} custom-call(bf16[128,8,1024]{2,1,0:T(8,128)(2,1)} %bitcast.15, bf16[128,8,1024]{2,1,0:T(8,128)(2,1)} %bitcast.13, bf16[128,8,1024]{2,1,0:T(8,128)(2,1)} %bitcast.14, bf16[128,8,1024]{2,1,0:T(8,128)(2,1)} %bitcast.16), custom_call_target="tpu_custom_call" | custom-call | bytes 8388608 | tf_op jit(solution)/shard_map/pack_columns/pallas_call | solution.py:118
  16.4 1.9 %pack_pairs.3 = bf16[2,1024,128]{2,1,0:T(8,128)(2,1)} custom-call(bf16[1,1024,1024]{2,1,0:T(8,128)(2,1)} %k_ref.10, bf16[1,1024,1024]{2,1,0:T(8,128)(2,1)} %v_ref.10), custom_call_target="tpu_custom_call" | custom-call | bytes 1048576 | tf_op jit(solution)/shard_map/pack_pairs/pallas_call | solution.py:80
  18.2 2.3 %collective-permute-start.1 = (bf16[2,1024,128]{2,1,0:T(8,128)(2,1)}, bf16[2,1024,128]{2,1,0:T(8,128)(2,1)}, u32[]{:S(2)}, u32[]{:S(2)}) collective-permute-start(bf16[2,1024,128]{2,1,0:T(8,128)(2,1)} %pack_pairs.3), channel_id=1, source_target_pairs={{0,1},{1,2},{2,3},{3,4},{4,5},{5,6},{6,7},{7,8},{8,9},{9,10},{10,1... | collective-permute-start | bytes 1572872 | tf_op jit(solution)/shard_map/ppermute | solution.py:406
  20.5 12.4 %all-to-all-start = ((bf16[128,4,8,512]{3,2,1,0:T(8,128)(2,1)}), bf16[128,4,8,512]{3,2,1,0:T(8,128)(2,1)}, u32[]{:S(2)}, u32[]{:S(2)}) async-start(bf16[128,4,8,512]{3,2,1,0:T(8,128)(2,1)} %pack_columns.1), calls=%async_computation | async-start | bytes 8388608 | tf_op jit(solution)/shard_map/all_to_all | solution.py:390
  33.0 9.1 %row_heads.4 = (bf16[1,1024,1024]{2,1,0:T(8,128)(2,1)}, bf16[1,1024,1024]{2,1,0:T(8,128)(2,1)}, bf16[1,1024,1024]{2,1,0:T(8,128)(2,1)}, bf16[1,1024,1024]{2,1,0:...) custom-call(f32[1]{0:T(128)} %bitcast.4.bias_ref, bf16[1,1024,1024]{2,1,0:T(8,128)(2,1)} %q_ref.7, ...), custom_call_target="tpu_custom_call" | custom-call | flops 167772160000 | bytes 3145728 | tf_op jit(solution)/shard_map/row_heads/pallas_call | solution.py:228
  42.1 0.0 collective-permute-done.3.prior_ref
  42.1 9.1 %row_heads.5 = (bf16[1,1024,1024]{2,1,0:T(8,128)(2,1)}, bf16[1,1024,1024]{2,1,0:T(8,128)(2,1)}, bf16[1,1024,1024]{2,1,0:T(8,128)(2,1)}, bf16[1,1024,1024]{2,1,0:...) custom-call(f32[1]{0:T(128)} %bitcast.4.bias_ref, ...), custom_call_target="tpu_custom_call", output_to_operand_aliasing={{0}: (6, {}), {1}: (7, {}), {2}: (8, {}), {3}: (9, {}), {4}... | custom-call | flops 167772160000 | bytes 3145728 | tf_op jit(solution)/shard_map/row_heads/pallas_call | solution.py:228
  51.2 0.0 collective-permute-done.2.prior_ref
  51.2 9.3 %row_heads.6 = (bf16[1,1024,1024]{2,1,0:T(8,128)(2,1)}, bf16[1,1024,1024]{2,1,0:T(8,128)(2,1)}, bf16[1,1024,1024]{2,1,0:T(8,128)(2,1)}, bf16[1,1024,1024]{2,1,0:...) custom-call(f32[1]{0:T(128)} %bitcast.4.bias_ref, ...), custom_call_target="tpu_custom_call", output_to_operand_aliasing={{0}: (6, {}), {1}: (7, {}), {2}: (8, {}), {3}: (9, {}), {4}... | custom-call | flops 167772160000 | bytes 3145728 | tf_op jit(solution)/shard_map/row_heads/pallas_call | solution.py:228
  60.5 9.1 %row_heads.7 = (bf16[1,1024,1024]{2,1,0:T(8,128)(2,1)}, bf16[1,1024,1024]{2,1,0:T(8,128)(2,1)}, bf16[1,1024,1024]{2,1,0:T(8,128)(2,1)}, bf16[1,1024,1024]{2,1,0:...) custom-call(f32[1]{0:T(128)} %bitcast.4.bias_ref, ...), custom_call_target="tpu_custom_call", output_to_operand_aliasing={{0}: (6, {}), {1}: (7, {}), {2}: (8, {}), {3}: (9, {}), {4}... | custom-call | flops 167772160000 | bytes 3145728 | tf_op jit(solution)/shard_map/row_heads/pallas_call | solution.py:228
  69.6 16.0 %all-to-all-done.in_ref = bf16[128,4,8,512]{3,2,1,0:T(8,128)(2,1)} async-done(((bf16[128,4,8,512]{3,2,1,0:T(8,128)(2,1)}), bf16[128,4,8,512]{3,2,1,0:T(8,128)(2,1)}, u32[]{:S(2)}, u32[]{:S(2)}) %all-to-all-start) | async-done | bytes 4194336 | tf_op jit(solution)/shard_map/all_to_all | solution.py:390
  85.6 2.8 %collective-permute-start.4 = (bf16[1,1024,512]{2,1,0:T(8,128)(2,1)}, bf16[1,1024,512]{2,1,0:T(8,128)(2,1)}, u32[]{:S(2)}, u32[]{:S(2)}) collective-permute-start(bf16[1,1024,512]{2,1,0:T(8,128)(2,1)} %get-tuple-element.71), channel_id=1, source_target_pairs={{1,0},{2,1},{3,2},{4,3},{5,4},{6,5},{7,6},{8,7},{9,8},{10,9},{11,1... | collective-permute-start | bytes 3145736 | tf_op jit(solution)/shard_map/ppermute | solution.py:417
  88.5 1.9 %collective-permute-start.5 = (bf16[1,1024,512]{2,1,0:T(8,128)(2,1)}, bf16[1,1024,512]{2,1,0:T(8,128)(2,1)}, u32[]{:S(2)}, u32[]{:S(2)}) collective-permute-start(bf16[1,1024,512]{2,1,0:T(8,128)(2,1)} %get-tuple-element.75), channel_id=1, source_target_pairs={{1,0},{2,1},{3,2},{4,3},{5,4},{6,5},{7,6},{8,7},{9,8},{10,9},{11,1... | collective-permute-start | bytes 3145736 | tf_op jit(solution)/shard_map/ppermute | solution.py:417
  90.4 8.0 %column_heads.1 = bf16[128,4,8,512]{3,2,1,0:T(8,128)(2,1)} custom-call(s32[128,1]{1,0:T(8,128)} %constant.24.row_down, s32[1,128]{1,0:T(1,128)} %constant.25.row_across, bf16[128,4,8,512]{3,2,1,0:T(8,128)(2,1)} %all-to-all-done.in_ref), custom_call_target="tpu_custom_call" | custom-call | flops 805306368 | bytes 8388608 | tf_op jit(solution)/shard_map/column_heads/pallas_call | solution.py:294
  98.4 3.6 %collective-permute-done.4.dk_back = bf16[1,1024,512]{2,1,0:T(8,128)(2,1)} collective-permute-done((bf16[1,1024,512]{2,1,0:T(8,128)(2,1)}, bf16[1,1024,512]{2,1,0:T(8,128)(2,1)}, u32[]{:S(2)}, u32[]{:S(2)}) %collective-permute-start.4) | collective-permute-done | bytes 1048608 | tf_op jit(solution)/shard_map/ppermute | solution.py:417
  102.0 7.4 %all-to-all-start.1 = ((bf16[128,4,8,512]{3,2,1,0:T(8,128)(2,1)}), bf16[128,4,8,512]{3,2,1,0:T(8,128)(2,1)}, u32[]{:S(2)}, u32[]{:S(2)}) async-start(bf16[128,4,8,512]{3,2,1,0:T(8,128)(2,1)} %column_heads.1), calls=%async_computation.1 | async-start | bytes 8388608 | tf_op jit(solution)/shard_map/all_to_all | solution.py:390
  109.4 37.0 %collective-permute-done.5.dv_back = bf16[1,1024,512]{2,1,0:T(8,128)(2,1)} collective-permute-done((bf16[1,1024,512]{2,1,0:T(8,128)(2,1)}, bf16[1,1024,512]{2,1,0:T(8,128)(2,1)}, u32[]{:S(2)}, u32[]{:S(2)}) %collective-permute-start.5) | collective-permute-done | bytes 1048608 | tf_op jit(solution)/shard_map/ppermute | solution.py:417
  146.4 3.3 %add_returned.1 = (bf16[1,1024,1024]{2,1,0:T(8,128)(2,1)}, bf16[1,1024,1024]{2,1,0:T(8,128)(2,1)}) custom-call(bf16[1,1024,512]{2,1,0:T(8,128)(2,1)} %collective-permute-done.4.dk_back, bf16[1,1024,512]{2,1,0:T(8,128)(2,1)} %collective-permute-done.5.dv_back, ...), custom_call_target="tpu_custom_call", output_to_operand_aliasing={{0}: (2, {}), {1}: (3, {})} | custom-call | flops 1677721600000 | bytes 6291456 | tf_op jit(solution)/shard_map/add_returned/pallas_call | solution.py:325
  149.7 12.4 %all-to-all-done.1.cols_ref = bf16[128,4,8,512]{3,2,1,0:T(8,128)(2,1)} async-done(((bf16[128,4,8,512]{3,2,1,0:T(8,128)(2,1)}), bf16[128,4,8,512]{3,2,1,0:T(8,128)(2,1)}, u32[]{:S(2)}, u32[]{:S(2)}) %all-to-all-start.1) | async-done | bytes 4194336 | tf_op jit(solution)/shard_map/all_to_all | solution.py:390
  162.1 3.4 %place.1 = (bf16[128,8,1024]{2,1,0:T(8,128)(2,1)}, bf16[128,8,1024]{2,1,0:T(8,128)(2,1)}, bf16[128,8,1024]{2,1,0:T(8,128)(2,1)}, bf16[128,8,1024]{2,1,0:T(8,128)(2,1)}) custom-call(bf16[128,4,8,512]{3,2,1,0:T(8,128)(2,1)} %all-to-all-done.1.cols_ref, ...), custom_call_target="tpu_custom_call", output_to_operand_aliasing={{0}: (1, {}), {1}: (2, {}), {2}: (3, {}), {3}: (4, {})} | custom-call | bytes 8388608 | tf_op jit(solution)/shard_map/place/pallas_call | solution.py:362
  (2 shorter events, 0.0 us)
Async XLA Ops:
  2.9 13.4 %collective-permute-start = (bf16[2,1024,128]{2,1,0:T(8,128)(2,1)}, bf16[2,1024,128]{2,1,0:T(8,128)(2,1)}, u32[]{:S(2)}, u32[]{:S(2)}) collective-permute-start(bf16[2,1024,128]{2,1,0:T(8,128)(2,1)} %get-tuple-element.44), channel_id=1, source_target_pairs={{0,1},{1,2},{2,3},{3,4},{4,5},{5,6},{6,7},{7,8},{8,9},{9,10},{10,1... | collective-permute-start | bytes 1572872 | tf_op jit(solution)/shard_map/ppermute | solution.py:403
  7.9 34.2 %collective-permute-start.3 = (bf16[2,1024,128]{2,1,0:T(8,128)(2,1)}, bf16[2,1024,128]{2,1,0:T(8,128)(2,1)}, u32[]{:S(2)}, u32[]{:S(2)}) collective-permute-start(bf16[2,1024,128]{2,1,0:T(8,128)(2,1)} %get-tuple-element.49), channel_id=1, source_target_pairs={{0,1},{1,2},{2,3},{3,4},{4,5},{5,6},{6,7},{7,8},{8,9},{9,10},{10,1... | collective-permute-start | bytes 1572872 | tf_op jit(solution)/shard_map/ppermute | solution.py:403
  9.8 41.4 %collective-permute-start.2 = (bf16[2,1024,128]{2,1,0:T(8,128)(2,1)}, bf16[2,1024,128]{2,1,0:T(8,128)(2,1)}, u32[]{:S(2)}, u32[]{:S(2)}) collective-permute-start(bf16[2,1024,128]{2,1,0:T(8,128)(2,1)} %get-tuple-element.48), channel_id=1, source_target_pairs={{0,1},{1,2},{2,3},{3,4},{4,5},{5,6},{6,7},{7,8},{8,9},{9,10},{10,1... | collective-permute-start | bytes 1572872 | tf_op jit(solution)/shard_map/ppermute | solution.py:403
  18.2 42.3 %collective-permute-start.1 = (bf16[2,1024,128]{2,1,0:T(8,128)(2,1)}, bf16[2,1024,128]{2,1,0:T(8,128)(2,1)}, u32[]{:S(2)}, u32[]{:S(2)}) collective-permute-start(bf16[2,1024,128]{2,1,0:T(8,128)(2,1)} %pack_pairs.3), channel_id=1, source_target_pairs={{0,1},{1,2},{2,3},{3,4},{4,5},{5,6},{6,7},{7,8},{8,9},{9,10},{10,1... | collective-permute-start | bytes 1572872 | tf_op jit(solution)/shard_map/ppermute | solution.py:406
  20.5 65.1 %all-to-all-start = ((bf16[128,4,8,512]{3,2,1,0:T(8,128)(2,1)}), bf16[128,4,8,512]{3,2,1,0:T(8,128)(2,1)}, u32[]{:S(2)}, u32[]{:S(2)}) async-start(bf16[128,4,8,512]{3,2,1,0:T(8,128)(2,1)} %pack_columns.1), calls=%async_computation | async-start | bytes 8388608 | tf_op jit(solution)/shard_map/all_to_all | solution.py:390
  85.6 16.4 %collective-permute-start.4 = (bf16[1,1024,512]{2,1,0:T(8,128)(2,1)}, bf16[1,1024,512]{2,1,0:T(8,128)(2,1)}, u32[]{:S(2)}, u32[]{:S(2)}) collective-permute-start(bf16[1,1024,512]{2,1,0:T(8,128)(2,1)} %get-tuple-element.71), channel_id=1, source_target_pairs={{1,0},{2,1},{3,2},{4,3},{5,4},{6,5},{7,6},{8,7},{9,8},{10,9},{11,1... | collective-permute-start | bytes 3145736 | tf_op jit(solution)/shard_map/ppermute | solution.py:417
  88.5 57.9 %collective-permute-start.5 = (bf16[1,1024,512]{2,1,0:T(8,128)(2,1)}, bf16[1,1024,512]{2,1,0:T(8,128)(2,1)}, u32[]{:S(2)}, u32[]{:S(2)}) collective-permute-start(bf16[1,1024,512]{2,1,0:T(8,128)(2,1)} %get-tuple-element.75), channel_id=1, source_target_pairs={{1,0},{2,1},{3,2},{4,3},{5,4},{6,5},{7,6},{8,7},{9,8},{10,9},{11,1... | collective-permute-start | bytes 3145736 | tf_op jit(solution)/shard_map/ppermute | solution.py:417
  102.0 60.0 %all-to-all-start.1 = ((bf16[128,4,8,512]{3,2,1,0:T(8,128)(2,1)}), bf16[128,4,8,512]{3,2,1,0:T(8,128)(2,1)}, u32[]{:S(2)}, u32[]{:S(2)}) async-start(bf16[128,4,8,512]{3,2,1,0:T(8,128)(2,1)} %column_heads.1), calls=%async_computation.1 | async-start | bytes 8388608 | tf_op jit(solution)/shard_map/all_to_all | solution.py:390
where the time goes:
time: 166 us
  waiting for transfers between devices  69 us (42%)
  Pallas kernels  59 us (36%)
  starting transfers between devices  36.8 us (22%)
    ppermute x2, waiting for transfers between devices, on_device(): back = [lax.ppermute(partial, AXES, backward) for partial in partials]  40.6 us
    pallas_call x4, Pallas kernels, row_heads(): pl.pallas_call(functools.partial(row_kernel, block, len(made)), grid=(hea...  36.6 us
    all_to_all x2, waiting for transfers between devices, exchange(): lax.all_to_all(blocks, AXES, split_axis=0, concat_axis=0, axis_index_grou...  28.4 us
    all_to_all x2, starting transfers between devices, exchange(): lax.all_to_all(blocks, AXES, split_axis=0, concat_axis=0, axis_index_grou...  19.8 us
    ppermute x3, starting transfers between devices, on_device(): prior = [lax.ppermute(pair, AXES, forward) for pair in pairs]  9.91 us
    pallas_call x1, Pallas kernels, column_heads(): pl.pallas_call(column_kernel, grid=(HALF,), in_specs=[pl.BlockSpec((rows,...  8.04 us
    ppermute x2, starting transfers between devices, on_device(): back = [lax.ppermute(partial, AXES, backward) for partial in partials]  4.75 us
    pallas_call x2, Pallas kernels, pack_pairs(): pl.pallas_call(functools.partial(pair_kernel, first), in_specs=[anywhere]...  4.13 us
  transfers between devices with their start and end apart: 8, of which 4 were waited for; matrix products, arithmetic and copies ran while one was open for 0% of the time, Pallas kernels for 32%

commit v1 on v0

--- a/solution.py
+++ b/solution.py
@@ -16,7 +16,7 @@
 LOG2E = math.log2(math.e)
 NEG = -1e30
 AHEAD = 1000
-PIECES = 4
+PIECES = 2
 CHUNKS = 4
 VMEM_BYTES = 64 * 1024 * 1024 - 256 * 1024
 AXES = ("grp", "seq")
@@ -60,12 +60,12 @@
         copy.wait()
 
 
-def pair_kernel(first, k_ref, v_ref, *refs):
+def pair_kernel(k_ref, v_ref, *refs):
     outs, (buffer, in_sems, out_sems) = refs[:-3], refs[-3:]
     wide = outs[0].shape[2]
     moves = []
     for piece, out in enumerate(outs):
-        here = pl.ds(first * HDIM + piece * wide, wide)
+        here = pl.ds(piece * wide, wide)
         incoming = [
             (ref.at[0, :, here], buffer.at[piece, at]) for at, ref in enumerate((k_ref, v_ref))
         ]
@@ -73,23 +73,23 @@
     stream(moves, in_sems, out_sems)
 
 
-def pack_pairs(key_vectors, value_vectors, first, pieces):
+def pack_pairs(key_vectors, value_vectors):
     _, length, width = key_vectors.shape
     wide = width // 2 // PIECES
     anywhere = pl.BlockSpec(memory_space=pl.ANY)
     return pl.pallas_call(
-        functools.partial(pair_kernel, first),
+        pair_kernel,
         in_specs=[anywhere] * 2,
-        out_specs=[anywhere] * pieces,
-        out_shape=[jax.ShapeDtypeStruct((2, length, wide), BF16)] * pieces,
+        out_specs=[anywhere] * PIECES,
+        out_shape=[jax.ShapeDtypeStruct((2, length, wide), BF16)] * PIECES,
         scratch_shapes=[
-            pltpu.VMEM((pieces, 2, length, wide), BF16),
-            pltpu.SemaphoreType.DMA((pieces, 2)),
-            pltpu.SemaphoreType.DMA((pieces, 1)),
+            pltpu.VMEM((PIECES, 2, length, wide), BF16),
+            pltpu.SemaphoreType.DMA((PIECES, 2)),
+            pltpu.SemaphoreType.DMA((PIECES, 1)),
         ],
         compiler_params=params(),
         cost_estimate=pl.CostEstimate(
-            flops=0, bytes_accessed=8 * pieces * length * wide, transcendentals=0
+            flops=0, bytes_accessed=8 * PIECES * length * wide, transcendentals=0
         ),
         name="pack_pairs",
     )(key_vectors, value_vectors)
@@ -381,7 +381,7 @@
 
 def exchange_order():
     order = []
-    for z_hi, z_lo, y, x, core in itertools.product(range(2), range(2), range(4), range(4), range(2)):
+    for z_hi, z_lo, core, y, x in itertools.product(range(2), range(2), range(2), range(4), range(4)):
         order.append(((z_hi * 4 + y) * 4 + x) * 4 + z_lo * 2 + core)
     return order
 
@@ -398,12 +398,8 @@
     arrays = (queries, key_vectors, value_vectors, out_cotangent)
     forward = [(i, i + 1) for i in range(devices - 1)]
     backward = [(i + 1, i) for i in range(devices - 1)]
-    last = PIECES - 1
-    pairs = pack_pairs(key_vectors, value_vectors, 0, last)
+    pairs = pack_pairs(key_vectors, value_vectors)
     prior = [lax.ppermute(pair, AXES, forward) for pair in pairs]
-    keys, values, _ = lax.optimization_barrier((key_vectors, value_vectors, prior[0]))
-    pair = pack_pairs(keys, values, last * (HALF // PIECES), 1)[0]
-    prior.append(lax.ppermute(pair, AXES, forward))
     packed = pack_columns(arrays, devices)
     packed, _ = lax.optimization_barrier((packed, prior[0]))
     arrived = exchange(packed, order)

time: 166 us -> 164 us (0.988)
  waiting for transfers between devices: 69 us -> 78.8 us
  Pallas kernels: 59 us -> 52.5 us
  starting transfers between devices: 36.8 us -> 30.8 us
    all_to_all x2, waiting for transfers between devices: 28.4 us -> 41.5 us  [exchange(): lax.all_to_all(blocks, AXES, split_axis=0, concat_axis=0, axis_index_grou...]
    ppermute x2, waiting for transfers between devices: 40.6 us -> 30.7 us  [on_device(): back = [lax.ppermute(partial, AXES, backward) for partial in partials]]
    ppermute x3 -> x2, waiting for transfers between devices: 0.01 us -> 6.62 us  [on_device(): prior = [lax.ppermute(pair, AXES, forward) for pair in pairs]]
    pallas_call x4 -> x2, Pallas kernels: 36.6 us -> 31.7 us  [row_heads(): pl.pallas_call(functools.partial(row_kernel, block, len(made)), grid=(hea...]
    ppermute x3 -> x2, starting transfers between devices: 9.91 us -> 6.86 us  [on_device(): prior = [lax.ppermute(pair, AXES, forward) for pair in pairs]]
    ppermute x1 -> x0, starting transfers between devices: 2.29 us -> none  [on_device(): prior.append(lax.ppermute(pair, AXES, forward))]
    pallas_call x2 -> x1, Pallas kernels: 4.13 us -> 2.57 us  [pack_pairs(): pl.pallas_call(pair_kernel, in_specs=[anywhere] * 2, out_specs=[anywhere]...]
  transfers between devices with their start and end apart: 8 -> 6, of which waited for: 4 -> 5; matrix products, arithmetic and copies ran while one was open for 0% -> 0% of each run, Pallas kernels for 32% -> 29%
where the time goes in v1:
time: 164 us; the launch traced here: 163 us
  waiting for transfers between devices  78.8 us (48%)
  Pallas kernels  52.5 us (32%)
  starting transfers between devices  30.8 us (19%)
    all_to_all x2, waiting for transfers between devices, exchange(): lax.all_to_all(blocks, AXES, split_axis=0, concat_axis=0, axis_index_grou...  41.5 us
    pallas_call x2, Pallas kernels, row_heads(): pl.pallas_call(functools.partial(row_kernel, block, len(made)), grid=(hea...  31.7 us
    ppermute x2, waiting for transfers between devices, on_device(): back = [lax.ppermute(partial, AXES, backward) for partial in partials]  30.7 us
    all_to_all x2, starting transfers between devices, exchange(): lax.all_to_all(blocks, AXES, split_axis=0, concat_axis=0, axis_index_grou...  19.7 us
    pallas_call x1, Pallas kernels, column_heads(): pl.pallas_call(column_kernel, grid=(HALF,), in_specs=[pl.BlockSpec((rows,...  8.04 us
    ppermute x2, starting transfers between devices, on_device(): prior = [lax.ppermute(pair, AXES, forward) for pair in pairs]  6.86 us
    ppermute x2, waiting for transfers between devices, on_device(): prior = [lax.ppermute(pair, AXES, forward) for pair in pairs]  6.62 us
    ppermute x2, starting transfers between devices, on_device(): back = [lax.ppermute(partial, AXES, backward) for partial in partials]  4.24 us
  transfers between devices with their start and end apart: 6, of which 5 were waited for; matrix products, arithmetic and copies ran while one was open for 0% of the time, Pallas kernels for 29%

profile of v1, /device:TPU:1, one launch (start us, length us, event | category | flops | bytes accessed | tf_op | source)
XLA Modules:
  0.0 163.0 jit_solution(6256781675515967899)
XLA Ops:
  0.6 2.6 %pack_pairs.1 = (bf16[2,1024,256]{2,1,0:T(8,128)(2,1)}, bf16[2,1024,256]{2,1,0:T(8,128)(2,1)}) custom-call(bf16[1,1024,1024]{2,1,0:T(8,128)(2,1)} %k_ref.5, bf16[1,1024,1024]{2,1,0:T(8,128)(2,1)} %v_ref.5), custom_call_target="tpu_custom_call" | custom-call | bytes 4194304 | tf_op jit(solution)/shard_map/pack_pairs/pallas_call | solution.py:80
  3.2 4.9 %collective-permute-start = (bf16[2,1024,256]{2,1,0:T(8,128)(2,1)}, bf16[2,1024,256]{2,1,0:T(8,128)(2,1)}, u32[]{:S(2)}, u32[]{:S(2)}) collective-permute-start(bf16[2,1024,256]{2,1,0:T(8,128)(2,1)} %get-tuple-element.29), channel_id=1, source_target_pairs={{0,1},{1,2},{2,3},{3,4},{4,5},{5,6},{6,7},{7,8},{8,9},{9,10},{10,1... | collective-permute-start | bytes 3145736 | tf_op jit(solution)/shard_map/ppermute | solution.py:402
  8.2 1.9 %collective-permute-start.1 = (bf16[2,1024,256]{2,1,0:T(8,128)(2,1)}, bf16[2,1024,256]{2,1,0:T(8,128)(2,1)}, u32[]{:S(2)}, u32[]{:S(2)}) collective-permute-start(bf16[2,1024,256]{2,1,0:T(8,128)(2,1)} %get-tuple-element.31), channel_id=1, source_target_pairs={{0,1},{1,2},{2,3},{3,4},{4,5},{5,6},{6,7},{7,8},{8,9},{9,10},{10,1... | collective-permute-start | bytes 3145736 | tf_op jit(solution)/shard_map/ppermute | solution.py:402
  10.1 3.5 %pack_columns.1 = bf16[128,4,8,512]{3,2,1,0:T(8,128)(2,1)} custom-call(bf16[128,8,1024]{2,1,0:T(8,128)(2,1)} %bitcast.15, bf16[128,8,1024]{2,1,0:T(8,128)(2,1)} %bitcast.13, bf16[128,8,1024]{2,1,0:T(8,128)(2,1)} %bitcast.14, bf16[128,8,1024]{2,1,0:T(8,128)(2,1)} %bitcast.16), custom_call_target="tpu_custom_call" | custom-call | bytes 8388608 | tf_op jit(solution)/shard_map/pack_columns/pallas_call | solution.py:118
  13.6 6.6 %collective-permute-done.prior_ref = bf16[2,1024,256]{2,1,0:T(8,128)(2,1)} collective-permute-done((bf16[2,1024,256]{2,1,0:T(8,128)(2,1)}, bf16[2,1024,256]{2,1,0:T(8,128)(2,1)}, u32[]{:S(2)}, u32[]{:S(2)}) %collective-permute-start) | collective-permute-done | bytes 1048608 | tf_op jit(solution)/shard_map/ppermute | solution.py:402
  20.2 12.1 %all-to-all-start = ((bf16[128,4,8,512]{3,2,1,0:T(8,128)(2,1)}), bf16[128,4,8,512]{3,2,1,0:T(8,128)(2,1)}, u32[]{:S(2)}, u32[]{:S(2)}) async-start(bf16[128,4,8,512]{3,2,1,0:T(8,128)(2,1)} %pack_columns.1), calls=%async_computation | async-start | bytes 8388608 | tf_op jit(solution)/shard_map/all_to_all | solution.py:390
  32.3 15.9 %row_heads.2 = (bf16[1,1024,1024]{2,1,0:T(8,128)(2,1)}, bf16[1,1024,1024]{2,1,0:T(8,128)(2,1)}, bf16[1,1024,1024]{2,1,0:T(8,128)(2,1)}, bf16[1,1024,1024]{2,1,0:...) custom-call(f32[1]{0:T(128)} %bitcast.4.bias_ref, bf16[1,1024,1024]{2,1,0:T(8,128)(2,1)} %q_ref.3, ...), custom_call_target="tpu_custom_call" | custom-call | flops 335544320000 | bytes 6291456 | tf_op jit(solution)/shard_map/row_heads/pallas_call | solution.py:228
  48.2 0.0 collective-permute-done.1.prior_ref
  48.2 15.9 %row_heads.3 = (bf16[1,1024,1024]{2,1,0:T(8,128)(2,1)}, bf16[1,1024,1024]{2,1,0:T(8,128)(2,1)}, bf16[1,1024,1024]{2,1,0:T(8,128)(2,1)}, bf16[1,1024,1024]{2,1,0:...) custom-call(f32[1]{0:T(128)} %bitcast.4.bias_ref, ...), custom_call_target="tpu_custom_call", output_to_operand_aliasing={{0}: (6, {}), {1}: (7, {}), {2}: (8, {}), {3}: (9, {}), {4}... | custom-call | flops 335544320000 | bytes 6291456 | tf_op jit(solution)/shard_map/row_heads/pallas_call | solution.py:228
  64.1 19.8 %all-to-all-done.in_ref = bf16[128,4,8,512]{3,2,1,0:T(8,128)(2,1)} async-done(((bf16[128,4,8,512]{3,2,1,0:T(8,128)(2,1)}), bf16[128,4,8,512]{3,2,1,0:T(8,128)(2,1)}, u32[]{:S(2)}, u32[]{:S(2)}) %all-to-all-start) | async-done | bytes 4194336 | tf_op jit(solution)/shard_map/all_to_all | solution.py:390
  83.9 2.3 %collective-permute-start.2 = (bf16[1,1024,512]{2,1,0:T(8,128)(2,1)}, bf16[1,1024,512]{2,1,0:T(8,128)(2,1)}, u32[]{:S(2)}, u32[]{:S(2)}) collective-permute-start(bf16[1,1024,512]{2,1,0:T(8,128)(2,1)} %get-tuple-element.41), channel_id=1, source_target_pairs={{1,0},{2,1},{3,2},{4,3},{5,4},{6,5},{7,6},{8,7},{9,8},{10,9},{11,1... | collective-permute-start | bytes 3145736 | tf_op jit(solution)/shard_map/ppermute | solution.py:413
  86.2 1.9 %collective-permute-start.3 = (bf16[1,1024,512]{2,1,0:T(8,128)(2,1)}, bf16[1,1024,512]{2,1,0:T(8,128)(2,1)}, u32[]{:S(2)}, u32[]{:S(2)}) collective-permute-start(bf16[1,1024,512]{2,1,0:T(8,128)(2,1)} %get-tuple-element.45), channel_id=1, source_target_pairs={{1,0},{2,1},{3,2},{4,3},{5,4},{6,5},{7,6},{8,7},{9,8},{10,9},{11,1... | collective-permute-start | bytes 3145736 | tf_op jit(solution)/shard_map/ppermute | solution.py:413
  88.1 8.0 %column_heads.1 = bf16[128,4,8,512]{3,2,1,0:T(8,128)(2,1)} custom-call(s32[128,1]{1,0:T(8,128)} %constant.24.row_down, s32[1,128]{1,0:T(1,128)} %constant.25.row_across, bf16[128,4,8,512]{3,2,1,0:T(8,128)(2,1)} %all-to-all-done.in_ref), custom_call_target="tpu_custom_call" | custom-call | flops 805306368 | bytes 8388608 | tf_op jit(solution)/shard_map/column_heads/pallas_call | solution.py:294
  96.2 4.1 %collective-permute-done.2.dk_back = bf16[1,1024,512]{2,1,0:T(8,128)(2,1)} collective-permute-done((bf16[1,1024,512]{2,1,0:T(8,128)(2,1)}, bf16[1,1024,512]{2,1,0:T(8,128)(2,1)}, u32[]{:S(2)}, u32[]{:S(2)}) %collective-permute-start.2) | collective-permute-done | bytes 1048608 | tf_op jit(solution)/shard_map/ppermute | solution.py:413
  100.3 7.6 %all-to-all-start.1 = ((bf16[128,4,8,512]{3,2,1,0:T(8,128)(2,1)}), bf16[128,4,8,512]{3,2,1,0:T(8,128)(2,1)}, u32[]{:S(2)}, u32[]{:S(2)}) async-start(bf16[128,4,8,512]{3,2,1,0:T(8,128)(2,1)} %column_heads.1), calls=%async_computation.1 | async-start | bytes 8388608 | tf_op jit(solution)/shard_map/all_to_all | solution.py:390
  107.9 26.5 %collective-permute-done.3.dv_back = bf16[1,1024,512]{2,1,0:T(8,128)(2,1)} collective-permute-done((bf16[1,1024,512]{2,1,0:T(8,128)(2,1)}, bf16[1,1024,512]{2,1,0:T(8,128)(2,1)}, u32[]{:S(2)}, u32[]{:S(2)}) %collective-permute-start.3) | collective-permute-done | bytes 1048608 | tf_op jit(solution)/shard_map/ppermute | solution.py:413
  134.4 3.3 %add_returned.1 = (bf16[1,1024,1024]{2,1,0:T(8,128)(2,1)}, bf16[1,1024,1024]{2,1,0:T(8,128)(2,1)}) custom-call(bf16[1,1024,512]{2,1,0:T(8,128)(2,1)} %collective-permute-done.2.dk_back, bf16[1,1024,512]{2,1,0:T(8,128)(2,1)} %collective-permute-done.3.dv_back, ...), custom_call_target="tpu_custom_call", output_to_operand_aliasing={{0}: (2, {}), {1}: (3, {})} | custom-call | flops 1677721600000 | bytes 6291456 | tf_op jit(solution)/shard_map/add_returned/pallas_call | solution.py:325
  137.7 21.7 %all-to-all-done.1.cols_ref = bf16[128,4,8,512]{3,2,1,0:T(8,128)(2,1)} async-done(((bf16[128,4,8,512]{3,2,1,0:T(8,128)(2,1)}), bf16[128,4,8,512]{3,2,1,0:T(8,128)(2,1)}, u32[]{:S(2)}, u32[]{:S(2)}) %all-to-all-start.1) | async-done | bytes 4194336 | tf_op jit(solution)/shard_map/all_to_all | solution.py:390
  159.4 3.4 %place.1 = (bf16[128,8,1024]{2,1,0:T(8,128)(2,1)}, bf16[128,8,1024]{2,1,0:T(8,128)(2,1)}, bf16[128,8,1024]{2,1,0:T(8,128)(2,1)}, bf16[128,8,1024]{2,1,0:T(8,128)(2,1)}) custom-call(bf16[128,4,8,512]{3,2,1,0:T(8,128)(2,1)} %all-to-all-done.1.cols_ref, ...), custom_call_target="tpu_custom_call", output_to_operand_aliasing={{0}: (1, {}), {1}: (2, {}), {2}: (3, {}), {3}: (4, {})} | custom-call | bytes 8388608 | tf_op jit(solution)/shard_map/place/pallas_call | solution.py:362
Async XLA Ops:
  3.2 17.0 %collective-permute-start = (bf16[2,1024,256]{2,1,0:T(8,128)(2,1)}, bf16[2,1024,256]{2,1,0:T(8,128)(2,1)}, u32[]{:S(2)}, u32[]{:S(2)}) collective-permute-start(bf16[2,1024,256]{2,1,0:T(8,128)(2,1)} %get-tuple-element.29), channel_id=1, source_target_pairs={{0,1},{1,2},{2,3},{3,4},{4,5},{5,6},{6,7},{7,8},{8,9},{9,10},{10,1... | collective-permute-start | bytes 3145736 | tf_op jit(solution)/shard_map/ppermute | solution.py:402
  8.2 40.1 %collective-permute-start.1 = (bf16[2,1024,256]{2,1,0:T(8,128)(2,1)}, bf16[2,1024,256]{2,1,0:T(8,128)(2,1)}, u32[]{:S(2)}, u32[]{:S(2)}) collective-permute-start(bf16[2,1024,256]{2,1,0:T(8,128)(2,1)} %get-tuple-element.31), channel_id=1, source_target_pairs={{0,1},{1,2},{2,3},{3,4},{4,5},{5,6},{6,7},{7,8},{8,9},{9,10},{10,1... | collective-permute-start | bytes 3145736 | tf_op jit(solution)/shard_map/ppermute | solution.py:402
  20.2 63.7 %all-to-all-start = ((bf16[128,4,8,512]{3,2,1,0:T(8,128)(2,1)}), bf16[128,4,8,512]{3,2,1,0:T(8,128)(2,1)}, u32[]{:S(2)}, u32[]{:S(2)}) async-start(bf16[128,4,8,512]{3,2,1,0:T(8,128)(2,1)} %pack_columns.1), calls=%async_computation | async-start | bytes 8388608 | tf_op jit(solution)/shard_map/all_to_all | solution.py:390
  83.9 16.4 %collective-permute-start.2 = (bf16[1,1024,512]{2,1,0:T(8,128)(2,1)}, bf16[1,1024,512]{2,1,0:T(8,128)(2,1)}, u32[]{:S(2)}, u32[]{:S(2)}) collective-permute-start(bf16[1,1024,512]{2,1,0:T(8,128)(2,1)} %get-tuple-element.41), channel_id=1, source_target_pairs={{1,0},{2,1},{3,2},{4,3},{5,4},{6,5},{7,6},{8,7},{9,8},{10,9},{11,1... | collective-permute-start | bytes 3145736 | tf_op jit(solution)/shard_map/ppermute | solution.py:413
  86.2 48.2 %collective-permute-start.3 = (bf16[1,1024,512]{2,1,0:T(8,128)(2,1)}, bf16[1,1024,512]{2,1,0:T(8,128)(2,1)}, u32[]{:S(2)}, u32[]{:S(2)}) collective-permute-start(bf16[1,1024,512]{2,1,0:T(8,128)(2,1)} %get-tuple-element.45), channel_id=1, source_target_pairs={{1,0},{2,1},{3,2},{4,3},{5,4},{6,5},{7,6},{8,7},{9,8},{10,9},{11,1... | collective-permute-start | bytes 3145736 | tf_op jit(solution)/shard_map/ppermute | solution.py:413
  100.3 59.1 %all-to-all-start.1 = ((bf16[128,4,8,512]{3,2,1,0:T(8,128)(2,1)}), bf16[128,4,8,512]{3,2,1,0:T(8,128)(2,1)}, u32[]{:S(2)}, u32[]{:S(2)}) async-start(bf16[128,4,8,512]{3,2,1,0:T(8,128)(2,1)} %column_heads.1), calls=%async_computation.1 | async-start | bytes 8388608 | tf_op jit(solution)/shard_map/all_to_all | solution.py:390

commit v2 on v1

--- a/solution.py
+++ b/solution.py
@@ -60,38 +60,34 @@
         copy.wait()
 
 
-def pair_kernel(k_ref, v_ref, *refs):
-    outs, (buffer, in_sems, out_sems) = refs[:-3], refs[-3:]
-    wide = outs[0].shape[2]
-    moves = []
-    for piece, out in enumerate(outs):
-        here = pl.ds(piece * wide, wide)
-        incoming = [
-            (ref.at[0, :, here], buffer.at[piece, at]) for at, ref in enumerate((k_ref, v_ref))
-        ]
-        moves.append((incoming, [(buffer.at[piece], out)]))
+def pair_kernel(first, k_ref, v_ref, out_ref, buffer, in_sems, out_sems):
+    here = pl.ds(first, out_ref.shape[2])
+    moves = [
+        ([(ref.at[0, :, here], buffer.at[at])], [(buffer.at[at], out_ref.at[at])])
+        for at, ref in enumerate((k_ref, v_ref))
+    ]
     stream(moves, in_sems, out_sems)
 
 
-def pack_pairs(key_vectors, value_vectors):
+def pack_pair(key_vectors, value_vectors, piece):
     _, length, width = key_vectors.shape
     wide = width // 2 // PIECES
     anywhere = pl.BlockSpec(memory_space=pl.ANY)
     return pl.pallas_call(
-        pair_kernel,
+        functools.partial(pair_kernel, piece * wide),
         in_specs=[anywhere] * 2,
-        out_specs=[anywhere] * PIECES,
-        out_shape=[jax.ShapeDtypeStruct((2, length, wide), BF16)] * PIECES,
+        out_specs=anywhere,
+        out_shape=jax.ShapeDtypeStruct((2, length, wide), BF16),
         scratch_shapes=[
-            pltpu.VMEM((PIECES, 2, length, wide), BF16),
-            pltpu.SemaphoreType.DMA((PIECES, 2)),
-            pltpu.SemaphoreType.DMA((PIECES, 1)),
+            pltpu.VMEM((2, length, wide), BF16),
+            pltpu.SemaphoreType.DMA((2, 1)),
+            pltpu.SemaphoreType.DMA((2, 1)),
         ],
         compiler_params=params(),
         cost_estimate=pl.CostEstimate(
-            flops=0, bytes_accessed=8 * PIECES * length * wide, transcendentals=0
-        ),
-        name="pack_pairs",
+            flops=0, bytes_accessed=8 * length * wide, transcendentals=0
+        ),
+        name="pack_pair",
     )(key_vectors, value_vectors)
 
 
@@ -258,7 +254,7 @@
     rows, _, per, _ = in_ref.shape
     staged, results = scratch[:4], scratch[4:]
     for at, ref in enumerate(staged):
-        ref[...] = in_ref[:, at].astype(F32).reshape(rows * per, HDIM)
+        ref[: rows * per] = in_ref[:, at].astype(F32).reshape(rows * per, HDIM)
     causal = row_down[...] <= row_across[...]
     factor = SCALING * LOG2E
     columns = range(per)
@@ -284,7 +280,7 @@
     for c in columns:
         results[2][picks[c], :] = matmul(dscore[c], query[c]) * SCALING
     for at, ref in enumerate(results):
-        out_ref[:, at] = ref[...].reshape(rows, per, HDIM).astype(BF16)
+        out_ref[:, at] = ref[: rows * per].reshape(rows, per, HDIM).astype(BF16)
 
 
 def column_heads(arrived, order):
@@ -301,7 +297,7 @@
         ],
         out_specs=spec,
         out_shape=jax.ShapeDtypeStruct(arrived.shape, BF16),
-        scratch_shapes=[pltpu.VMEM((rows * per, HDIM), F32)] * 8,
+        scratch_shapes=[pltpu.VMEM((rows * per + per, HDIM), F32)] * 8,
         compiler_params=params(),
         cost_estimate=pl.CostEstimate(
             flops=12 * HALF * per * rows * rows * HDIM,
@@ -398,8 +394,13 @@
     arrays = (queries, key_vectors, value_vectors, out_cotangent)
     forward = [(i, i + 1) for i in range(devices - 1)]
     backward = [(i + 1, i) for i in range(devices - 1)]
-    pairs = pack_pairs(key_vectors, value_vectors)
-    prior = [lax.ppermute(pair, AXES, forward) for pair in pairs]
+    prior, pair = [], None
+    for piece in range(PIECES):
+        sources = (key_vectors, value_vectors)
+        if pair is not None:
+            *sources, _ = lax.optimization_barrier((*sources, pair))
+        pair = pack_pair(*sources, piece)
+        prior.append(lax.ppermute(pair, AXES, forward))
     packed = pack_columns(arrays, devices)
     packed, _ = lax.optimization_barrier((packed, prior[0]))
     arrived = exchange(packed, order)

time: 164 us -> 163 us (level)
  waiting for transfers between devices: 78.8 us -> 76.7 us
    ppermute x2, waiting for transfers between devices: 6.62 us -> 4.57 us  [on_device(): prior.append(lax.ppermute(pair, AXES, forward))]
    pallas_call x1 -> x2, Pallas kernels: 2.57 us -> 4.08 us  [pack_pair(): pl.pallas_call(functools.partial(pair_kernel, piece * wide), in_specs=[an...]
  transfers between devices with their start and end apart: 6 -> 6, of which waited for: 5 -> 5; matrix products, arithmetic and copies ran while one was open for 0% -> 0% of each run, Pallas kernels for 29% -> 30%
where the time goes in v2:
time: 163 us; the launch traced here: 162 us
  waiting for transfers between devices  76.7 us (47%)
  Pallas kernels  54 us (33%)
  starting transfers between devices  30.8 us (19%)
    all_to_all x2, waiting for transfers between devices, exchange(): lax.all_to_all(blocks, AXES, split_axis=0, concat_axis=0, axis_index_grou...  41.5 us
    pallas_call x2, Pallas kernels, row_heads(): pl.pallas_call(functools.partial(row_kernel, block, len(made)), grid=(hea...  31.7 us
    ppermute x2, waiting for transfers between devices, on_device(): back = [lax.ppermute(partial, AXES, backward) for partial in partials]  30.7 us
    all_to_all x2, starting transfers between devices, exchange(): lax.all_to_all(blocks, AXES, split_axis=0, concat_axis=0, axis_index_grou...  19.7 us
    pallas_call x1, Pallas kernels, column_heads(): pl.pallas_call(column_kernel, grid=(HALF,), in_specs=[pl.BlockSpec((rows,...  8.04 us
    ppermute x2, starting transfers between devices, on_device(): prior.append(lax.ppermute(pair, AXES, forward))  6.86 us
    ppermute x2, waiting for transfers between devices, on_device(): prior.append(lax.ppermute(pair, AXES, forward))  4.57 us
    ppermute x2, starting transfers between devices, on_device(): back = [lax.ppermute(partial, AXES, backward) for partial in partials]  4.24 us
  transfers between devices with their start and end apart: 6, of which 5 were waited for; matrix products, arithmetic and copies ran while one was open for 0% of the time, Pallas kernels for 30%

profile of v2, /device:TPU:1, one launch (start us, length us, event | category | flops | bytes accessed | tf_op | source)
XLA Modules:
  0.0 162.4 jit_solution(17254918013819139737)
XLA Ops:
  0.6 2.0 %pack_pair.2 = bf16[2,1024,256]{2,1,0:T(8,128)(2,1)} custom-call(bf16[1,1024,1024]{2,1,0:T(8,128)(2,1)} %k_ref.6, bf16[1,1024,1024]{2,1,0:T(8,128)(2,1)} %v_ref.6), custom_call_target="tpu_custom_call" | custom-call | bytes 2097152 | tf_op jit(solution)/shard_map/pack_pair/pallas_call | solution.py:76
  2.7 4.9 %collective-permute-start = (bf16[2,1024,256]{2,1,0:T(8,128)(2,1)}, bf16[2,1024,256]{2,1,0:T(8,128)(2,1)}, u32[]{:S(2)}, u32[]{:S(2)}) collective-permute-start(bf16[2,1024,256]{2,1,0:T(8,128)(2,1)} %pack_pair.2), channel_id=1, source_target_pairs={{0,1},{1,2},{2,3},{3,4},{4,5},{5,6},{6,7},{7,8},{8,9},{9,10},{10,1... | collective-permute-start | bytes 3145736 | tf_op jit(solution)/shard_map/ppermute | solution.py:403
  7.6 2.0 %pack_pair.3 = bf16[2,1024,256]{2,1,0:T(8,128)(2,1)} custom-call(bf16[1,1024,1024]{2,1,0:T(8,128)(2,1)} %k_ref.6, bf16[1,1024,1024]{2,1,0:T(8,128)(2,1)} %v_ref.6), custom_call_target="tpu_custom_call" | custom-call | bytes 2097152 | tf_op jit(solution)/shard_map/pack_pair/pallas_call | solution.py:76
  9.7 1.9 %collective-permute-start.1 = (bf16[2,1024,256]{2,1,0:T(8,128)(2,1)}, bf16[2,1024,256]{2,1,0:T(8,128)(2,1)}, u32[]{:S(2)}, u32[]{:S(2)}) collective-permute-start(bf16[2,1024,256]{2,1,0:T(8,128)(2,1)} %pack_pair.3), channel_id=1, source_target_pairs={{0,1},{1,2},{2,3},{3,4},{4,5},{5,6},{6,7},{7,8},{8,9},{9,10},{10,1... | collective-permute-start | bytes 3145736 | tf_op jit(solution)/shard_map/ppermute | solution.py:403
  11.6 3.5 %pack_columns.1 = bf16[128,4,8,512]{3,2,1,0:T(8,128)(2,1)} custom-call(bf16[128,8,1024]{2,1,0:T(8,128)(2,1)} %bitcast.15, bf16[128,8,1024]{2,1,0:T(8,128)(2,1)} %bitcast.13, bf16[128,8,1024]{2,1,0:T(8,128)(2,1)} %bitcast.14, bf16[128,8,1024]{2,1,0:T(8,128)(2,1)} %bitcast.16), custom_call_target="tpu_custom_call" | custom-call | bytes 8388608 | tf_op jit(solution)/shard_map/pack_columns/pallas_call | solution.py:114
  15.1 4.6 %collective-permute-done.prior_ref = bf16[2,1024,256]{2,1,0:T(8,128)(2,1)} collective-permute-done((bf16[2,1024,256]{2,1,0:T(8,128)(2,1)}, bf16[2,1024,256]{2,1,0:T(8,128)(2,1)}, u32[]{:S(2)}, u32[]{:S(2)}) %collective-permute-start) | collective-permute-done | bytes 1048608 | tf_op jit(solution)/shard_map/ppermute | solution.py:403
  19.7 12.1 %all-to-all-start = ((bf16[128,4,8,512]{3,2,1,0:T(8,128)(2,1)}), bf16[128,4,8,512]{3,2,1,0:T(8,128)(2,1)}, u32[]{:S(2)}, u32[]{:S(2)}) async-start(bf16[128,4,8,512]{3,2,1,0:T(8,128)(2,1)} %pack_columns.1), calls=%async_computation | async-start | bytes 8388608 | tf_op jit(solution)/shard_map/all_to_all | solution.py:386
  31.8 15.9 %row_heads.2 = (bf16[1,1024,1024]{2,1,0:T(8,128)(2,1)}, bf16[1,1024,1024]{2,1,0:T(8,128)(2,1)}, bf16[1,1024,1024]{2,1,0:T(8,128)(2,1)}, bf16[1,1024,1024]{2,1,0:...) custom-call(f32[1]{0:T(128)} %bitcast.4.bias_ref, bf16[1,1024,1024]{2,1,0:T(8,128)(2,1)} %q_ref.3, ...), custom_call_target="tpu_custom_call" | custom-call | flops 335544320000 | bytes 6291456 | tf_op jit(solution)/shard_map/row_heads/pallas_call | solution.py:224
  47.7 0.0 collective-permute-done.1.prior_ref
  47.7 15.9 %row_heads.3 = (bf16[1,1024,1024]{2,1,0:T(8,128)(2,1)}, bf16[1,1024,1024]{2,1,0:T(8,128)(2,1)}, bf16[1,1024,1024]{2,1,0:T(8,128)(2,1)}, bf16[1,1024,1024]{2,1,0:...) custom-call(f32[1]{0:T(128)} %bitcast.4.bias_ref, ...), custom_call_target="tpu_custom_call", output_to_operand_aliasing={{0}: (6, {}), {1}: (7, {}), {2}: (8, {}), {3}: (9, {}), {4}... | custom-call | flops 335544320000 | bytes 6291456 | tf_op jit(solution)/shard_map/row_heads/pallas_call | solution.py:224
  63.6 19.8 %all-to-all-done.in_ref = bf16[128,4,8,512]{3,2,1,0:T(8,128)(2,1)} async-done(((bf16[128,4,8,512]{3,2,1,0:T(8,128)(2,1)}), bf16[128,4,8,512]{3,2,1,0:T(8,128)(2,1)}, u32[]{:S(2)}, u32[]{:S(2)}) %all-to-all-start) | async-done | bytes 4194336 | tf_op jit(solution)/shard_map/all_to_all | solution.py:386
  83.4 2.3 %collective-permute-start.2 = (bf16[1,1024,512]{2,1,0:T(8,128)(2,1)}, bf16[1,1024,512]{2,1,0:T(8,128)(2,1)}, u32[]{:S(2)}, u32[]{:S(2)}) collective-permute-start(bf16[1,1024,512]{2,1,0:T(8,128)(2,1)} %get-tuple-element.41), channel_id=1, source_target_pairs={{1,0},{2,1},{3,2},{4,3},{5,4},{6,5},{7,6},{8,7},{9,8},{10,9},{11,1... | collective-permute-start | bytes 3145736 | tf_op jit(solution)/shard_map/ppermute | solution.py:414
  85.7 1.9 %collective-permute-start.3 = (bf16[1,1024,512]{2,1,0:T(8,128)(2,1)}, bf16[1,1024,512]{2,1,0:T(8,128)(2,1)}, u32[]{:S(2)}, u32[]{:S(2)}) collective-permute-start(bf16[1,1024,512]{2,1,0:T(8,128)(2,1)} %get-tuple-element.45), channel_id=1, source_target_pairs={{1,0},{2,1},{3,2},{4,3},{5,4},{6,5},{7,6},{8,7},{9,8},{10,9},{11,1... | collective-permute-start | bytes 3145736 | tf_op jit(solution)/shard_map/ppermute | solution.py:414
  87.6 8.0 %column_heads.1 = bf16[128,4,8,512]{3,2,1,0:T(8,128)(2,1)} custom-call(s32[128,1]{1,0:T(8,128)} %constant.24.row_down, s32[1,128]{1,0:T(1,128)} %constant.25.row_across, bf16[128,4,8,512]{3,2,1,0:T(8,128)(2,1)} %all-to-all-done.in_ref), custom_call_target="tpu_custom_call" | custom-call | flops 805306368 | bytes 8388608 | tf_op jit(solution)/shard_map/column_heads/pallas_call | solution.py:290
  95.6 4.1 %collective-permute-done.2.dk_back = bf16[1,1024,512]{2,1,0:T(8,128)(2,1)} collective-permute-done((bf16[1,1024,512]{2,1,0:T(8,128)(2,1)}, bf16[1,1024,512]{2,1,0:T(8,128)(2,1)}, u32[]{:S(2)}, u32[]{:S(2)}) %collective-permute-start.2) | collective-permute-done | bytes 1048608 | tf_op jit(solution)/shard_map/ppermute | solution.py:414
  99.8 7.6 %all-to-all-start.1 = ((bf16[128,4,8,512]{3,2,1,0:T(8,128)(2,1)}), bf16[128,4,8,512]{3,2,1,0:T(8,128)(2,1)}, u32[]{:S(2)}, u32[]{:S(2)}) async-start(bf16[128,4,8,512]{3,2,1,0:T(8,128)(2,1)} %column_heads.1), calls=%async_computation.1 | async-start | bytes 8388608 | tf_op jit(solution)/shard_map/all_to_all | solution.py:386
  107.4 26.5 %collective-permute-done.3.dv_back = bf16[1,1024,512]{2,1,0:T(8,128)(2,1)} collective-permute-done((bf16[1,1024,512]{2,1,0:T(8,128)(2,1)}, bf16[1,1024,512]{2,1,0:T(8,128)(2,1)}, u32[]{:S(2)}, u32[]{:S(2)}) %collective-permute-start.3) | collective-permute-done | bytes 1048608 | tf_op jit(solution)/shard_map/ppermute | solution.py:414
  133.9 3.3 %add_returned.1 = (bf16[1,1024,1024]{2,1,0:T(8,128)(2,1)}, bf16[1,1024,1024]{2,1,0:T(8,128)(2,1)}) custom-call(bf16[1,1024,512]{2,1,0:T(8,128)(2,1)} %collective-permute-done.2.dk_back, bf16[1,1024,512]{2,1,0:T(8,128)(2,1)} %collective-permute-done.3.dv_back, ...), custom_call_target="tpu_custom_call", output_to_operand_aliasing={{0}: (2, {}), {1}: (3, {})} | custom-call | flops 1677721600000 | bytes 6291456 | tf_op jit(solution)/shard_map/add_returned/pallas_call | solution.py:321
  137.2 21.7 %all-to-all-done.1.cols_ref = bf16[128,4,8,512]{3,2,1,0:T(8,128)(2,1)} async-done(((bf16[128,4,8,512]{3,2,1,0:T(8,128)(2,1)}), bf16[128,4,8,512]{3,2,1,0:T(8,128)(2,1)}, u32[]{:S(2)}, u32[]{:S(2)}) %all-to-all-start.1) | async-done | bytes 4194336 | tf_op jit(solution)/shard_map/all_to_all | solution.py:386
  158.9 3.4 %place.1 = (bf16[128,8,1024]{2,1,0:T(8,128)(2,1)}, bf16[128,8,1024]{2,1,0:T(8,128)(2,1)}, bf16[128,8,1024]{2,1,0:T(8,128)(2,1)}, bf16[128,8,1024]{2,1,0:T(8,128)(2,1)}) custom-call(bf16[128,4,8,512]{3,2,1,0:T(8,128)(2,1)} %all-to-all-done.1.cols_ref, ...), custom_call_target="tpu_custom_call", output_to_operand_aliasing={{0}: (1, {}), {1}: (2, {}), {2}: (3, {}), {3}: (4, {})} | custom-call | bytes 8388608 | tf_op jit(solution)/shard_map/place/pallas_call | solution.py:358
Async XLA Ops:
  2.7 17.0 %collective-permute-start = (bf16[2,1024,256]{2,1,0:T(8,128)(2,1)}, bf16[2,1024,256]{2,1,0:T(8,128)(2,1)}, u32[]{:S(2)}, u32[]{:S(2)}) collective-permute-start(bf16[2,1024,256]{2,1,0:T(8,128)(2,1)} %pack_pair.2), channel_id=1, source_target_pairs={{0,1},{1,2},{2,3},{3,4},{4,5},{5,6},{6,7},{7,8},{8,9},{9,10},{10,1... | collective-permute-start | bytes 3145736 | tf_op jit(solution)/shard_map/ppermute | solution.py:403
  9.7 38.0 %collective-permute-start.1 = (bf16[2,1024,256]{2,1,0:T(8,128)(2,1)}, bf16[2,1024,256]{2,1,0:T(8,128)(2,1)}, u32[]{:S(2)}, u32[]{:S(2)}) collective-permute-start(bf16[2,1024,256]{2,1,0:T(8,128)(2,1)} %pack_pair.3), channel_id=1, source_target_pairs={{0,1},{1,2},{2,3},{3,4},{4,5},{5,6},{6,7},{7,8},{8,9},{9,10},{10,1... | collective-permute-start | bytes 3145736 | tf_op jit(solution)/shard_map/ppermute | solution.py:403
  19.7 63.7 %all-to-all-start = ((bf16[128,4,8,512]{3,2,1,0:T(8,128)(2,1)}), bf16[128,4,8,512]{3,2,1,0:T(8,128)(2,1)}, u32[]{:S(2)}, u32[]{:S(2)}) async-start(bf16[128,4,8,512]{3,2,1,0:T(8,128)(2,1)} %pack_columns.1), calls=%async_computation | async-start | bytes 8388608 | tf_op jit(solution)/shard_map/all_to_all | solution.py:386
  83.4 16.4 %collective-permute-start.2 = (bf16[1,1024,512]{2,1,0:T(8,128)(2,1)}, bf16[1,1024,512]{2,1,0:T(8,128)(2,1)}, u32[]{:S(2)}, u32[]{:S(2)}) collective-permute-start(bf16[1,1024,512]{2,1,0:T(8,128)(2,1)} %get-tuple-element.41), channel_id=1, source_target_pairs={{1,0},{2,1},{3,2},{4,3},{5,4},{6,5},{7,6},{8,7},{9,8},{10,9},{11,1... | collective-permute-start | bytes 3145736 | tf_op jit(solution)/shard_map/ppermute | solution.py:414
  85.7 48.2 %collective-permute-start.3 = (bf16[1,1024,512]{2,1,0:T(8,128)(2,1)}, bf16[1,1024,512]{2,1,0:T(8,128)(2,1)}, u32[]{:S(2)}, u32[]{:S(2)}) collective-permute-start(bf16[1,1024,512]{2,1,0:T(8,128)(2,1)} %get-tuple-element.45), channel_id=1, source_target_pairs={{1,0},{2,1},{3,2},{4,3},{5,4},{6,5},{7,6},{8,7},{9,8},{10,9},{11,1... | collective-permute-start | bytes 3145736 | tf_op jit(solution)/shard_map/ppermute | solution.py:414
  99.8 59.1 %all-to-all-start.1 = ((bf16[128,4,8,512]{3,2,1,0:T(8,128)(2,1)}), bf16[128,4,8,512]{3,2,1,0:T(8,128)(2,1)}, u32[]{:S(2)}, u32[]{:S(2)}) async-start(bf16[128,4,8,512]{3,2,1,0:T(8,128)(2,1)} %column_heads.1), calls=%async_computation.1 | async-start | bytes 8388608 | tf_op jit(solution)/shard_map/all_to_all | solution.py:386

commit v3 on v2

--- a/solution.py
+++ b/solution.py
@@ -377,7 +377,7 @@
 
 def exchange_order():
     order = []
-    for z_hi, z_lo, core, y, x in itertools.product(range(2), range(2), range(2), range(4), range(4)):
+    for z_hi, core, z_lo, y, x in itertools.product(range(2), range(2), range(2), range(4), range(4)):
         order.append(((z_hi * 4 + y) * 4 + x) * 4 + z_lo * 2 + core)
     return order
 

time: 163 us -> 163 us (level)
  waiting for transfers between devices: 76.7 us -> 74.9 us
    ppermute x2, waiting for transfers between devices: 30.7 us -> 17 us  [on_device(): back = [lax.ppermute(partial, AXES, backward) for partial in partials]]
    all_to_all x2, waiting for transfers between devices: 41.5 us -> 53.3 us  [exchange(): lax.all_to_all(blocks, AXES, split_axis=0, concat_axis=0, axis_index_grou...]
where the time goes in v3:
time: 163 us; the launch traced here: 162 us
  waiting for transfers between devices  74.9 us (46%)
  Pallas kernels  54 us (33%)
  starting transfers between devices  32.4 us (20%)
    all_to_all x2, waiting for transfers between devices, exchange(): lax.all_to_all(blocks, AXES, split_axis=0, concat_axis=0, axis_index_grou...  53.3 us
    pallas_call x2, Pallas kernels, row_heads(): pl.pallas_call(functools.partial(row_kernel, block, len(made)), grid=(hea...  31.7 us
    all_to_all x2, starting transfers between devices, exchange(): lax.all_to_all(blocks, AXES, split_axis=0, concat_axis=0, axis_index_grou...  20.4 us
    ppermute x2, waiting for transfers between devices, on_device(): back = [lax.ppermute(partial, AXES, backward) for partial in partials]  17 us
    pallas_call x1, Pallas kernels, column_heads(): pl.pallas_call(column_kernel, grid=(HALF,), in_specs=[pl.BlockSpec((rows,...  8.05 us
    ppermute x2, starting transfers between devices, on_device(): prior.append(lax.ppermute(pair, AXES, forward))  6.86 us
    ppermute x2, starting transfers between devices, on_device(): back = [lax.ppermute(partial, AXES, backward) for partial in partials]  5.14 us
    ppermute x2, waiting for transfers between devices, on_device(): prior.append(lax.ppermute(pair, AXES, forward))  4.57 us
  transfers between devices with their start and end apart: 6, of which 5 were waited for; matrix products, arithmetic and copies ran while one was open for 0% of the time, Pallas kernels for 30%

profile of v3, /device:TPU:1, one launch (start us, length us, event | category | flops | bytes accessed | tf_op | source)
XLA Modules:
  0.0 162.2 jit_solution(13686556245316437988)
XLA Ops:
  0.6 2.0 %pack_pair.2 = bf16[2,1024,256]{2,1,0:T(8,128)(2,1)} custom-call(bf16[1,1024,1024]{2,1,0:T(8,128)(2,1)} %k_ref.6, bf16[1,1024,1024]{2,1,0:T(8,128)(2,1)} %v_ref.6), custom_call_target="tpu_custom_call" | custom-call | bytes 2097152 | tf_op jit(solution)/shard_map/pack_pair/pallas_call | solution.py:76
  2.7 4.9 %collective-permute-start = (bf16[2,1024,256]{2,1,0:T(8,128)(2,1)}, bf16[2,1024,256]{2,1,0:T(8,128)(2,1)}, u32[]{:S(2)}, u32[]{:S(2)}) collective-permute-start(bf16[2,1024,256]{2,1,0:T(8,128)(2,1)} %pack_pair.2), channel_id=1, source_target_pairs={{0,1},{1,2},{2,3},{3,4},{4,5},{5,6},{6,7},{7,8},{8,9},{9,10},{10,1... | collective-permute-start | bytes 3145736 | tf_op jit(solution)/shard_map/ppermute | solution.py:403
  7.6 2.0 %pack_pair.3 = bf16[2,1024,256]{2,1,0:T(8,128)(2,1)} custom-call(bf16[1,1024,1024]{2,1,0:T(8,128)(2,1)} %k_ref.6, bf16[1,1024,1024]{2,1,0:T(8,128)(2,1)} %v_ref.6), custom_call_target="tpu_custom_call" | custom-call | bytes 2097152 | tf_op jit(solution)/shard_map/pack_pair/pallas_call | solution.py:76
  9.7 1.9 %collective-permute-start.1 = (bf16[2,1024,256]{2,1,0:T(8,128)(2,1)}, bf16[2,1024,256]{2,1,0:T(8,128)(2,1)}, u32[]{:S(2)}, u32[]{:S(2)}) collective-permute-start(bf16[2,1024,256]{2,1,0:T(8,128)(2,1)} %pack_pair.3), channel_id=1, source_target_pairs={{0,1},{1,2},{2,3},{3,4},{4,5},{5,6},{6,7},{7,8},{8,9},{9,10},{10,1... | collective-permute-start | bytes 3145736 | tf_op jit(solution)/shard_map/ppermute | solution.py:403
  11.6 3.5 %pack_columns.1 = bf16[128,4,8,512]{3,2,1,0:T(8,128)(2,1)} custom-call(bf16[128,8,1024]{2,1,0:T(8,128)(2,1)} %bitcast.15, bf16[128,8,1024]{2,1,0:T(8,128)(2,1)} %bitcast.13, bf16[128,8,1024]{2,1,0:T(8,128)(2,1)} %bitcast.14, bf16[128,8,1024]{2,1,0:T(8,128)(2,1)} %bitcast.16), custom_call_target="tpu_custom_call" | custom-call | bytes 8388608 | tf_op jit(solution)/shard_map/pack_columns/pallas_call | solution.py:114
  15.1 4.6 %collective-permute-done.prior_ref = bf16[2,1024,256]{2,1,0:T(8,128)(2,1)} collective-permute-done((bf16[2,1024,256]{2,1,0:T(8,128)(2,1)}, bf16[2,1024,256]{2,1,0:T(8,128)(2,1)}, u32[]{:S(2)}, u32[]{:S(2)}) %collective-permute-start) | collective-permute-done | bytes 1048608 | tf_op jit(solution)/shard_map/ppermute | solution.py:403
  19.7 12.1 %all-to-all-start = ((bf16[128,4,8,512]{3,2,1,0:T(8,128)(2,1)}), bf16[128,4,8,512]{3,2,1,0:T(8,128)(2,1)}, u32[]{:S(2)}, u32[]{:S(2)}) async-start(bf16[128,4,8,512]{3,2,1,0:T(8,128)(2,1)} %pack_columns.1), calls=%async_computation | async-start | bytes 8388608 | tf_op jit(solution)/shard_map/all_to_all | solution.py:386
  31.8 15.9 %row_heads.2 = (bf16[1,1024,1024]{2,1,0:T(8,128)(2,1)}, bf16[1,1024,1024]{2,1,0:T(8,128)(2,1)}, bf16[1,1024,1024]{2,1,0:T(8,128)(2,1)}, bf16[1,1024,1024]{2,1,0:...) custom-call(f32[1]{0:T(128)} %bitcast.4.bias_ref, bf16[1,1024,1024]{2,1,0:T(8,128)(2,1)} %q_ref.3, ...), custom_call_target="tpu_custom_call" | custom-call | flops 335544320000 | bytes 6291456 | tf_op jit(solution)/shard_map/row_heads/pallas_call | solution.py:224
  47.7 0.0 collective-permute-done.1.prior_ref
  47.7 15.9 %row_heads.3 = (bf16[1,1024,1024]{2,1,0:T(8,128)(2,1)}, bf16[1,1024,1024]{2,1,0:T(8,128)(2,1)}, bf16[1,1024,1024]{2,1,0:T(8,128)(2,1)}, bf16[1,1024,1024]{2,1,0:...) custom-call(f32[1]{0:T(128)} %bitcast.4.bias_ref, ...), custom_call_target="tpu_custom_call", output_to_operand_aliasing={{0}: (6, {}), {1}: (7, {}), {2}: (8, {}), {3}: (9, {}), {4}... | custom-call | flops 335544320000 | bytes 6291456 | tf_op jit(solution)/shard_map/row_heads/pallas_call | solution.py:224
  63.6 19.3 %all-to-all-done.in_ref = bf16[128,4,8,512]{3,2,1,0:T(8,128)(2,1)} async-done(((bf16[128,4,8,512]{3,2,1,0:T(8,128)(2,1)}), bf16[128,4,8,512]{3,2,1,0:T(8,128)(2,1)}, u32[]{:S(2)}, u32[]{:S(2)}) %all-to-all-start) | async-done | bytes 4194336 | tf_op jit(solution)/shard_map/all_to_all | solution.py:386
  82.9 3.2 %collective-permute-start.2 = (bf16[1,1024,512]{2,1,0:T(8,128)(2,1)}, bf16[1,1024,512]{2,1,0:T(8,128)(2,1)}, u32[]{:S(2)}, u32[]{:S(2)}) collective-permute-start(bf16[1,1024,512]{2,1,0:T(8,128)(2,1)} %get-tuple-element.41), channel_id=1, source_target_pairs={{1,0},{2,1},{3,2},{4,3},{5,4},{6,5},{7,6},{8,7},{9,8},{10,9},{11,1... | collective-permute-start | bytes 3145736 | tf_op jit(solution)/shard_map/ppermute | solution.py:414
  86.1 1.9 %collective-permute-start.3 = (bf16[1,1024,512]{2,1,0:T(8,128)(2,1)}, bf16[1,1024,512]{2,1,0:T(8,128)(2,1)}, u32[]{:S(2)}, u32[]{:S(2)}) collective-permute-start(bf16[1,1024,512]{2,1,0:T(8,128)(2,1)} %get-tuple-element.45), channel_id=1, source_target_pairs={{1,0},{2,1},{3,2},{4,3},{5,4},{6,5},{7,6},{8,7},{9,8},{10,9},{11,1... | collective-permute-start | bytes 3145736 | tf_op jit(solution)/shard_map/ppermute | solution.py:414
  88.1 8.0 %column_heads.1 = bf16[128,4,8,512]{3,2,1,0:T(8,128)(2,1)} custom-call(s32[128,1]{1,0:T(8,128)} %constant.24.row_down, s32[1,128]{1,0:T(1,128)} %constant.25.row_across, bf16[128,4,8,512]{3,2,1,0:T(8,128)(2,1)} %all-to-all-done.in_ref), custom_call_target="tpu_custom_call" | custom-call | flops 805306368 | bytes 8388608 | tf_op jit(solution)/shard_map/column_heads/pallas_call | solution.py:290
  96.1 3.2 %collective-permute-done.2.dk_back = bf16[1,1024,512]{2,1,0:T(8,128)(2,1)} collective-permute-done((bf16[1,1024,512]{2,1,0:T(8,128)(2,1)}, bf16[1,1024,512]{2,1,0:T(8,128)(2,1)}, u32[]{:S(2)}, u32[]{:S(2)}) %collective-permute-start.2) | collective-permute-done | bytes 1048608 | tf_op jit(solution)/shard_map/ppermute | solution.py:414
  99.3 8.3 %all-to-all-start.1 = ((bf16[128,4,8,512]{3,2,1,0:T(8,128)(2,1)}), bf16[128,4,8,512]{3,2,1,0:T(8,128)(2,1)}, u32[]{:S(2)}, u32[]{:S(2)}) async-start(bf16[128,4,8,512]{3,2,1,0:T(8,128)(2,1)} %column_heads.1), calls=%async_computation.1 | async-start | bytes 8388608 | tf_op jit(solution)/shard_map/all_to_all | solution.py:386
  107.6 13.8 %collective-permute-done.3.dv_back = bf16[1,1024,512]{2,1,0:T(8,128)(2,1)} collective-permute-done((bf16[1,1024,512]{2,1,0:T(8,128)(2,1)}, bf16[1,1024,512]{2,1,0:T(8,128)(2,1)}, u32[]{:S(2)}, u32[]{:S(2)}) %collective-permute-start.3) | collective-permute-done | bytes 1048608 | tf_op jit(solution)/shard_map/ppermute | solution.py:414
  121.4 3.3 %add_returned.1 = (bf16[1,1024,1024]{2,1,0:T(8,128)(2,1)}, bf16[1,1024,1024]{2,1,0:T(8,128)(2,1)}) custom-call(bf16[1,1024,512]{2,1,0:T(8,128)(2,1)} %collective-permute-done.2.dk_back, bf16[1,1024,512]{2,1,0:T(8,128)(2,1)} %collective-permute-done.3.dv_back, ...), custom_call_target="tpu_custom_call", output_to_operand_aliasing={{0}: (2, {}), {1}: (3, {})} | custom-call | flops 1677721600000 | bytes 6291456 | tf_op jit(solution)/shard_map/add_returned/pallas_call | solution.py:321
  124.7 34.0 %all-to-all-done.1.cols_ref = bf16[128,4,8,512]{3,2,1,0:T(8,128)(2,1)} async-done(((bf16[128,4,8,512]{3,2,1,0:T(8,128)(2,1)}), bf16[128,4,8,512]{3,2,1,0:T(8,128)(2,1)}, u32[]{:S(2)}, u32[]{:S(2)}) %all-to-all-start.1) | async-done | bytes 4194336 | tf_op jit(solution)/shard_map/all_to_all | solution.py:386
  158.7 3.4 %place.1 = (bf16[128,8,1024]{2,1,0:T(8,128)(2,1)}, bf16[128,8,1024]{2,1,0:T(8,128)(2,1)}, bf16[128,8,1024]{2,1,0:T(8,128)(2,1)}, bf16[128,8,1024]{2,1,0:T(8,128)(2,1)}) custom-call(bf16[128,4,8,512]{3,2,1,0:T(8,128)(2,1)} %all-to-all-done.1.cols_ref, ...), custom_call_target="tpu_custom_call", output_to_operand_aliasing={{0}: (1, {}), {1}: (2, {}), {2}: (3, {}), {3}: (4, {})} | custom-call | bytes 8388608 | tf_op jit(solution)/shard_map/place/pallas_call | solution.py:358
Async XLA Ops:
  2.7 17.0 %collective-permute-start = (bf16[2,1024,256]{2,1,0:T(8,128)(2,1)}, bf16[2,1024,256]{2,1,0:T(8,128)(2,1)}, u32[]{:S(2)}, u32[]{:S(2)}) collective-permute-start(bf16[2,1024,256]{2,1,0:T(8,128)(2,1)} %pack_pair.2), channel_id=1, source_target_pairs={{0,1},{1,2},{2,3},{3,4},{4,5},{5,6},{6,7},{7,8},{8,9},{9,10},{10,1... | collective-permute-start | bytes 3145736 | tf_op jit(solution)/shard_map/ppermute | solution.py:403
  9.7 38.0 %collective-permute-start.1 = (bf16[2,1024,256]{2,1,0:T(8,128)(2,1)}, bf16[2,1024,256]{2,1,0:T(8,128)(2,1)}, u32[]{:S(2)}, u32[]{:S(2)}) collective-permute-start(bf16[2,1024,256]{2,1,0:T(8,128)(2,1)} %pack_pair.3), channel_id=1, source_target_pairs={{0,1},{1,2},{2,3},{3,4},{4,5},{5,6},{6,7},{7,8},{8,9},{9,10},{10,1... | collective-permute-start | bytes 3145736 | tf_op jit(solution)/shard_map/ppermute | solution.py:403
  19.7 63.2 %all-to-all-start = ((bf16[128,4,8,512]{3,2,1,0:T(8,128)(2,1)}), bf16[128,4,8,512]{3,2,1,0:T(8,128)(2,1)}, u32[]{:S(2)}, u32[]{:S(2)}) async-start(bf16[128,4,8,512]{3,2,1,0:T(8,128)(2,1)} %pack_columns.1), calls=%async_computation | async-start | bytes 8388608 | tf_op jit(solution)/shard_map/all_to_all | solution.py:386
  82.9 16.4 %collective-permute-start.2 = (bf16[1,1024,512]{2,1,0:T(8,128)(2,1)}, bf16[1,1024,512]{2,1,0:T(8,128)(2,1)}, u32[]{:S(2)}, u32[]{:S(2)}) collective-permute-start(bf16[1,1024,512]{2,1,0:T(8,128)(2,1)} %get-tuple-element.41), channel_id=1, source_target_pairs={{1,0},{2,1},{3,2},{4,3},{5,4},{6,5},{7,6},{8,7},{9,8},{10,9},{11,1... | collective-permute-start | bytes 3145736 | tf_op jit(solution)/shard_map/ppermute | solution.py:414
  86.1 35.3 %collective-permute-start.3 = (bf16[1,1024,512]{2,1,0:T(8,128)(2,1)}, bf16[1,1024,512]{2,1,0:T(8,128)(2,1)}, u32[]{:S(2)}, u32[]{:S(2)}) collective-permute-start(bf16[1,1024,512]{2,1,0:T(8,128)(2,1)} %get-tuple-element.45), channel_id=1, source_target_pairs={{1,0},{2,1},{3,2},{4,3},{5,4},{6,5},{7,6},{8,7},{9,8},{10,9},{11,1... | collective-permute-start | bytes 3145736 | tf_op jit(solution)/shard_map/ppermute | solution.py:414
  99.3 59.4 %all-to-all-start.1 = ((bf16[128,4,8,512]{3,2,1,0:T(8,128)(2,1)}), bf16[128,4,8,512]{3,2,1,0:T(8,128)(2,1)}, u32[]{:S(2)}, u32[]{:S(2)}) async-start(bf16[128,4,8,512]{3,2,1,0:T(8,128)(2,1)} %column_heads.1), calls=%async_computation.1 | async-start | bytes 8388608 | tf_op jit(solution)/shard_map/all_to_all | solution.py:386
